TPU v7x, 32 devices: a whole 2x2x4 slice. The times are simulated.
32 devices in a mesh: leaf: 8 (over z, y), col: 4 (over x, core).
Axes of the slice: x: 2, y: 2, z: 4, core: 2. Of those that a mesh axis runs over, the one named last changes fastest.
Arguments:
- child_fronts: float32 [8, 2048, 2048], P('leaf', 'col'), may hold values from -8 to 8, as said below
- child_index: int32 [8, 6], replicated, may hold values from 0 to 23, as said below
- parent_front: float32 [6144, 6144], P('leaf', 'col'), may hold values from -8 to 8, as said below
Outputs:
- child_factor: float32 [8, 2048, 512], P('leaf', 'col')
- parent_factor: float32 [6144, 6144], P('leaf', 'col')
Inputs may be any that keep to these rules, and one draw needn't show every extreme that they name: `child_index`: in each row the 6 indices are distinct and so are their groups index // 3; hence one row names at most 2 indices in any aligned group of 6 blocks (blocks 6k to 6k+5), and exactly 2 in some. `child_fronts`: each child front is symmetric with diagonal entries of 0.5 to 7 and smallest eigenvalue above 0.5. `parent_front`: symmetric with diagonal entries of 0.5 to 7 and smallest eigenvalue above 0.5.
All inputs are finite; a program needn't handle non-finite values.
Results may differ from a plain program's by a relative error of at most 0.00016.
Values sent between devices are 32-bit elements; how exact they have to be, the bound alone decides.
A program may use at most 192 MiB of HBM per device.

v0:
```python
import jax
import jax.numpy as jnp
from jax import lax
from jax.sharding import PartitionSpec as P

B = 256
PC = 2
ROWBLK = 3


highest = lax.Precision.HIGHEST


def spread_2(shard, axis, root):
    mine = lax.axis_index(axis) == root
    return lax.psum(jnp.where(mine, shard, jnp.zeros_like(shard)), axis)


def solve_rows(factor, rows):
    return jax.scipy.linalg.solve_triangular(factor, rows.T, lower=True).T


def route_slots(indices, col_blocks):
    target = indices // col_blocks
    count = indices.shape[-1]
    earlier_mask = lax.broadcasted_iota(jnp.int32, (count, count), 1) < lax.broadcasted_iota(
        jnp.int32, (count, count), 0
    )
    same = target[..., :, None] == target[..., None, :]
    ranking = jnp.sum((same & earlier_mask).astype(jnp.int32), axis=-1)
    return (target, ranking)


def per_device(child_fronts, child_index, parent_front):
    leaf_pos = lax.axis_index("leaf")
    col_pos = lax.axis_index("col")
    leaf_count = lax.axis_size("leaf")
    col_count = lax.axis_size("col")
    share = leaf_count // col_count
    children = child_index.shape[0]
    contrib_count = child_index.shape[1]
    front_rows = child_fronts[0]
    row_count = front_rows.shape[0]
    pivot_width = PC * B
    raw_panel = front_rows[:, :pivot_width]
    whole_panel = lax.all_gather(raw_panel, "col", axis=0, tiled=True)
    pivot_factor = jnp.linalg.cholesky(whole_panel[:pivot_width])
    solved_all = solve_rows(pivot_factor, whole_panel)
    own_rows = lax.dynamic_slice_in_dim(solved_all, col_pos * row_count, row_count, 0)
    first_device = col_pos == 0
    child_out = jnp.where(first_device, pivot_factor, own_rows)[None]
    update_rows = front_rows[:, pivot_width:] - jnp.dot(
        own_rows, solved_all[pivot_width:].T, precision=highest, preferred_element_type=jnp.float32
    )
    update_rows = jnp.where(first_device, 0.0, update_rows)
    col_blocks = ROWBLK * leaf_count // col_count
    own_index = lax.dynamic_index_in_dim(child_index, leaf_pos, 0, keepdims=False)
    target, ranking = route_slots(own_index, col_blocks)
    slot_ids = jnp.arange(col_count * share, dtype=jnp.int32)
    selector = (slot_ids[:, None] == (target * share + ranking)[None, :]).astype(jnp.float32)
    selector = selector.reshape(col_count, share, contrib_count)
    pieces = update_rows.reshape(row_count, contrib_count, B)
    outgoing = jnp.einsum("msc,rcb->mrsb", selector, pieces, precision=highest)
    incoming = lax.all_to_all(outgoing, "col", split_axis=0, concat_axis=0, tiled=True)
    columns = incoming.reshape(col_count * row_count, share * B)
    contrib_rows = columns[pivot_width:].reshape(contrib_count, B, share * B)
    leaf_target = own_index // ROWBLK
    row_select = (jnp.arange(leaf_count, dtype=jnp.int32)[:, None] == leaf_target[None, :]).astype(
        jnp.float32
    )
    outgoing_rows = jnp.einsum("lr,rbx->lbx", row_select, contrib_rows, precision=highest)
    arrived = lax.all_to_all(outgoing_rows, "leaf", split_axis=0, concat_axis=0, tiled=True)
    all_target, all_rank = route_slots(child_index, col_blocks)
    local_col = child_index - col_pos * col_blocks
    hits = (all_target == col_pos)[:, :, None, None]
    hits = hits & (
        all_rank[:, :, None, None] == jnp.arange(share, dtype=jnp.int32)[None, None, :, None]
    )
    hits = hits & (
        local_col[:, :, None, None] == jnp.arange(col_blocks, dtype=jnp.int32)[None, None, None, :]
    )
    col_select = jnp.sum(hits.astype(jnp.float32), axis=1)
    local_row = child_index - leaf_pos * ROWBLK
    row_place = jnp.sum(
        (local_row[:, :, None] == jnp.arange(ROWBLK, dtype=jnp.int32)[None, None, :]).astype(
            jnp.float32
        ),
        axis=1,
    )
    arrived_blocks = arrived.reshape(children, B, share, B)
    spread = jnp.einsum("gsq,gbse->gbqe", col_select, arrived_blocks, precision=highest)
    update = jnp.einsum("gp,gbqe->pbqe", row_place, spread, precision=highest)
    assembled = parent_front + update.reshape(ROWBLK * B, col_blocks * B)
    parent_pivots = ROWBLK * B
    raw_rows = spread_2(assembled[:, :parent_pivots], "col", 0)
    received = []
    for turn in range(share + 1):
        root = col_pos * 0 if turn == 0 else col_pos * share + turn - 1
        received.append(spread_2(raw_rows, "leaf", root))
    parent_pivot = jnp.linalg.cholesky(received[0])
    row_panel = solve_rows(parent_pivot, raw_rows)
    col_panel = solve_rows(parent_pivot, jnp.concatenate(received[1:], 0))
    schur = assembled - jnp.dot(
        row_panel, col_panel.T, precision=highest, preferred_element_type=jnp.float32
    )
    left = jnp.where(leaf_pos == 0, parent_pivot, row_panel)
    left_full = jnp.concatenate(
        [left, jnp.zeros((left.shape[0], assembled.shape[1] - parent_pivots), jnp.float32)], 1
    )
    global_row = leaf_pos * assembled.shape[0] + lax.broadcasted_iota(jnp.int32, assembled.shape, 0)
    global_col = col_pos * assembled.shape[1] + lax.broadcasted_iota(jnp.int32, assembled.shape, 1)
    parent_out = jnp.where(
        global_col < parent_pivots, left_full, jnp.where(global_row < parent_pivots, 0.0, schur)
    )
    return (child_out, parent_out)


def solution(mesh):
    placed = (P("leaf", "col", None), P(), P("leaf", "col"))
    return jax.shard_map(
        per_device,
        mesh=mesh,
        in_specs=placed,
        out_specs=(P("leaf", "col", None), P("leaf", "col")),
        check_vma=False,
    )
```

profile of v0, /device:TPU:0, one launch (start us, length us, event | category | flops | bytes accessed | tf_op | source)
XLA Modules:
  0.0 1055.5 jit_solution(13163752814835611861)
XLA Ops:
  15.1 37.0 %all-gather.2.cloned.1.call-done = f32[2048,512]{0,1:T(8,128)} async-done(((f32[512,512]{0,1:T(8,128)}), f32[2048,512]{0,1:T(8,128)}) %all-gather.2.cloned.1.call-update) | async-done | bytes 4194320 | tf_op jit(solution)/shard_map/all_gather | solution.py:46
  55.2 11.7 %cholesky.221 = f32[128,128]{1,0:T(8,128)S(1)} custom-call(f32[128,128]{1,0:T(8,128)S(1)} %cholesky.570), custom_call_target="Cholesky" | custom-call | tf_op jit(solution)/shard_map/jit(cholesky)/cholesky | solution.py:47
  67.1 9.8 custom-call.67
  77.6 11.7 %cholesky.235 = f32[128,128]{1,0:T(8,128)S(1)} custom-call(f32[128,128]{1,0:T(8,128)S(1)} %cholesky.574), custom_call_target="Cholesky" | custom-call | tf_op jit(solution)/shard_map/jit(cholesky)/cholesky | solution.py:47
  89.3 10.0 custom-call.68
  100.0 11.7 %cholesky.254 = f32[128,128]{1,0:T(8,128)S(1)} custom-call(f32[128,128]{1,0:T(8,128)S(1)} %cholesky.579), custom_call_target="Cholesky" | custom-call | tf_op jit(solution)/shard_map/jit(cholesky)/cholesky | solution.py:47
  111.8 9.8 custom-call.69
  122.2 11.7 %cholesky.462 = f32[128,128]{1,0:T(8,128)S(1)} custom-call(f32[128,128]{1,0:T(8,128)S(1)} %convolution_subtract_fusion.18), custom_call_target="Cholesky" | custom-call | tf_op jit(solution)/shard_map/jit(cholesky)/cholesky | solution.py:47
  134.9 10.9 %compare_reduce_fusion.6 = pred[]{:T(512)} fusion(f32[128]{0:T(128)S(1)} %get-tuple-element.108), kind=kLoop, calls=%fused_computation.256 | loop fusion | flops 255 | bytes 513 | tf_op jit(solution)/shard_map/jit(cholesky)/cholesky | solution.py:47
  149.2 10.9 %while.2 = (s32[]{:T(128)}, f32[512,512]{1,0:T(8,128)S(1)}, s32[4,2]{0,1:T(2,128)S(1)}, f32[4,128,128]{2,1,0:T(8,128)}, s32[]{:T(128)}) while((s32[]{:T(128)}, f32[512,512]{1,0:T(8,128)S(1)}, s32[4,2]{0,1:T(2,128)S(1)}, f32[4,128,128]{2,1,0:T(8,128)}, s32[]{:T(128)}) %tuple.86), condition=%wide.while_cond, body=%wide.while_body.sunk | while | flops 2 | bytes 132205 | solution.py:20
  160.1 40.2 %custom-call.60 = f32[4,128,128]{1,2,0:T(8,128)S(1)} custom-call(f32[4,128,128]{2,1,0:T(8,128)} %get-tuple-element.12), custom_call_target="InvertDiagBlocksLowerTriangular" | custom-call | tf_op jit(solution)/shard_map/jit(_solve_triangular)/triangular_solve | solution.py:20
  247.4 48.2 %all-to-all-done = f32[4,512,2,256]{3,2,1,0:T(2,128)} async-done(((f32[4,512,2,256]{3,2,1,0:T(2,128)}), f32[4,512,2,256]{3,2,1,0:T(2,128)}, u32[]{:S(2)}, u32[]{:S(2)}) %all-to-all-start) | async-done | bytes 4194336 | tf_op jit(solution)/shard_map/all_to_all | solution.py:64
  325.0 86.0 %all-to-all-done.1 = f32[8,256,512]{2,1,0:T(8,128)} async-done(((f32[8,256,512]{2,1,0:T(8,128)}), f32[8,256,512]{2,1,0:T(8,128)}, u32[]{:S(2)}, u32[]{:S(2)}) %all-to-all-start.1) | async-done | bytes 4194336 | tf_op jit(solution)/shard_map/all_to_all | solution.py:72
  416.9 19.5 %convolution_bitcast_fusion = f32[8,256,6,256]{3,2,1,0:T(8,128)S(1)} fusion(f32[8,256,2,256]{3,2,1,0:T(2,128)} %reshape.200, f32[8,2,6,1]{2,1,3,0:T(2,128)S(1)} %copy.128), kind=kOutput, calls=%fused_computation.6 | convolution fusion | flops 75497472 | bytes 16777600 | tf_op jit(solution)/shard_map/gsq,gbse->gbqe/dot_general | solution.py:91
  436.4 18.1 %fusion = f32[3,256,6,256]{3,0,2,1:T(4,128)} fusion(f32[8,256,6,256]{3,2,1,0:T(8,128)S(1)} %convolution_bitcast_fusion, f32[8,3]{0,1:T(4,128)S(1)} %convert_reduce_fusion.1), kind=kOutput, calls=%fused_computation.4 | convolution fusion | flops 113246208 | bytes 17301600 | tf_op jit(solution)/shard_map/gp,gbqe->pbqe/dot_general | solution.py:92
  454.5 8.7 copy.136
  473.9 53.9 %all-reduce.7.cloned.1.call-done = f32[768,768]{0,1:T(8,128)} async-done(((f32[768,768]{0,1:T(8,128)}), f32[768,768]{0,1:T(8,128)}) %all-reduce.7.cloned.1.call-update) | async-done | bytes 2359312 | tf_op jit(solution)/shard_map/psum | solution.py:16
  536.1 231.9 %all-reduce.9.cloned.1.call-done = (f32[768,768]{0,1:T(8,128)}, f32[768,768]{0,1:T(8,128)}, f32[768,768]{0,1:T(8,128)}) async-done(((f32[768,768]{0,1:T(8,128)}, f32[768,768]{0,1:T(8,128)}, f32[768,768]{0,1:T(8,128)}), (f32[768,768]{0,1:T(8,128)}, f32[768,768]{0,1:T(8,128)}, f32[768,768]{0,1:T(8,128)})) %all-reduce.9.cloned.1.call-update) | async-done | bytes 7077904 | tf_op jit(solution)/shard_map/psum | solution.py:16
  775.1 11.7 %cholesky.474 = f32[128,128]{1,0:T(8,128)S(1)} custom-call(f32[128,128]{1,0:T(8,128)S(1)} %cholesky.583), custom_call_target="Cholesky" | custom-call | tf_op jit(solution)/shard_map/jit(cholesky)/cholesky | solution.py:100
  786.9 9.8 custom-call.61
  799.7 11.7 %cholesky.492 = f32[128,128]{1,0:T(8,128)S(1)} custom-call(f32[128,128]{1,0:T(8,128)S(1)} %cholesky.587), custom_call_target="Cholesky" | custom-call | tf_op jit(solution)/shard_map/jit(cholesky)/cholesky | solution.py:100
  811.7 10.0 custom-call.62
  824.1 11.7 %cholesky.513 = f32[128,128]{1,0:T(8,128)S(1)} custom-call(f32[128,128]{1,0:T(8,128)S(1)} %cholesky.592), custom_call_target="Cholesky" | custom-call | tf_op jit(solution)/shard_map/jit(cholesky)/cholesky | solution.py:100
  836.0 9.8 custom-call.70
  848.3 12.1 %cholesky.528 = f32[128,128]{1,0:T(8,128)S(1)} custom-call(f32[128,128]{1,0:T(8,128)S(1)} %cholesky.597), custom_call_target="Cholesky" | custom-call | tf_op jit(solution)/shard_map/jit(cholesky)/cholesky | solution.py:100
  860.5 9.8 custom-call.71
  872.6 11.7 %cholesky.543 = f32[128,128]{1,0:T(8,128)S(1)} custom-call(f32[128,128]{1,0:T(8,128)S(1)} %cholesky.602), custom_call_target="Cholesky" | custom-call | tf_op jit(solution)/shard_map/jit(cholesky)/cholesky | solution.py:100
  884.5 9.8 custom-call.72
  896.3 11.7 %cholesky.557 = f32[128,128]{1,0:T(8,128)S(1)} custom-call(f32[128,128]{1,0:T(8,128)S(1)} %convolution_subtract_fusion.17), custom_call_target="Cholesky" | custom-call | tf_op jit(solution)/shard_map/jit(cholesky)/cholesky | solution.py:100
  917.8 22.1 %while.3 = (s32[]{:T(128)}, f32[768,768]{0,1:T(8,128)}, s32[6,2]{0,1:T(2,128)S(1)}, f32[6,128,128]{2,1,0:T(8,128)}, s32[]{:T(128)}) while((s32[]{:T(128)}, f32[768,768]{0,1:T(8,128)}, s32[6,2]{0,1:T(2,128)S(1)}, f32[6,128,128]{2,1,0:T(8,128)}, s32[]{:T(128)}) %tuple.89), condition=%wide.while_cond.1, body=%wide.while_body.1.sunk | while | flops 2 | bytes 393329 | solution.py:20
  939.8 59.8 %custom-call.63 = f32[6,128,128]{1,2,0:T(8,128)S(1)} custom-call(f32[6,128,128]{2,1,0:T(8,128)} %get-tuple-element.20), custom_call_target="InvertDiagBlocksLowerTriangular" | custom-call | tf_op jit(solution)/shard_map/jit(_solve_triangular)/triangular_solve | solution.py:20
  1026.9 15.6 %select_select_fusion = f32[768,1536]{0,1:T(8,128)} fusion(f32[768,1536]{0,1:T(8,128)S(1)} %bitcast.227, f32[768,768]{0,1:T(8,128)S(1)} %bitcast_select_fusion, f32[768,768]{1,0:T(8,128)S(1)} %convolution_dynamic-update-slice_fusion.1, f32[768,1536]{1,0:T(8,128)S(1)} %convolution_dynamic-update-slice_fusion, pred[1536]{0:T(1024)(128)(4,1)S(1)} %add_compare_fusion, ...), kind=kOutput, calls=%fused_computation.8 | convolution fusion | flops 10875174912 | bytes 18876672 | tf_op jit(solution)/shard_map/dot_general | solution.py:103
  (231 shorter events, 207.6 us)
Async XLA Ops:
  7.2 45.0 %all-gather.2.cloned.1.call-start = ((), (), s32[]{:S(2)}) async-start(), calls=%async_computation.2 | async-start | bytes 5242880 | tf_op jit(solution)/shard_map/all_gather | solution.py:46
  12.6 2.3 copy-start.15
  52.2 1.2 slice-start.2
  134.0 66.3 %copy-start.2 = (f32[512,512]{1,0:T(8,128)}, f32[512,512]{1,0:T(8,128)S(1)}, u32[]{:S(2)}) copy-start(f32[512,512]{1,0:T(8,128)S(1)} %get-tuple-element.109) | copy-start | bytes 3145732
  160.1 45.9 %copy-start.12 = (f32[512,512]{1,0:T(8,128)}, f32[512,512]{1,0:T(8,128)S(1)}, u32[]{:S(2)}) copy-start(f32[512,512]{1,0:T(8,128)S(1)} %get-tuple-element.245) | copy-start | bytes 3145732
  202.6 3.5 copy-start.6
  214.0 4.5 copy-start.10
  215.3 3.1 copy-start.11
  218.5 3.7 copy-start.1
  219.1 8.8 copy-start.5
  242.1 53.5 %all-to-all-start = ((f32[4,512,2,256]{3,2,1,0:T(2,128)}), f32[4,512,2,256]{3,2,1,0:T(2,128)}, u32[]{:S(2)}, u32[]{:S(2)}) async-start(f32[4,512,2,256]{3,2,1,0:T(2,128)} %copy.99), calls=%async_computation | async-start | bytes 8388608 | tf_op jit(solution)/shard_map/all_to_all | solution.py:64
  312.4 98.6 %all-to-all-start.1 = ((f32[8,256,512]{2,1,0:T(8,128)}), f32[8,256,512]{2,1,0:T(8,128)}, u32[]{:S(2)}, u32[]{:S(2)}) async-start(f32[8,256,512]{2,1,0:T(8,128)} %copy.101), calls=%async_computation.1 | async-start | bytes 8388608 | tf_op jit(solution)/shard_map/all_to_all | solution.py:72
  317.9 209.9 %all-reduce.7.cloned.1.call-start = ((), (), s32[]{:S(2)}) async-start(), calls=%async_computation.3 | async-start | bytes 4718592 | tf_op jit(solution)/shard_map/psum | solution.py:16
  470.1 2.2 copy-start
  473.9 294.2 %all-reduce.9.cloned.1.call-start = ((), (), s32[]{:S(2)}) async-start(), calls=%async_computation.4 | async-start | bytes 14155776 | tf_op jit(solution)/shard_map/psum | solution.py:16
  532.5 1.2 copy-start.3
  768.0 3.6 copy-start.4
  773.6 1.5 copy-start.9
  999.6 3.8 copy-start.7
  1002.8 2.8 copy-start.8
  1010.5 1.7 copy-start.13
  1010.5 2.4 copy-start.14
  1020.9 6.0 slice-start
  1022.8 4.2 slice-start.1
Sparse Core Ops, SparseCore 0:
  15.0 37.1 all-gather.1
  474.0 53.8 all-reduce.6
  532.7 235.3 all-reduce.8
where the time goes:
time: 1070 us; the launch traced here: 1060 us
  waiting for transfers between devices  457 us (43%)
  other arithmetic  332 us (31%)
  matrix products  122 us (11%)
  local copies, waits for them, and re-layouts  112 us (10%)
  between operations  21.7 us (2%)
  starting transfers between devices  10.9 us (1%)
    psum x2, waiting for transfers between devices, spread_2(): return lax.psum(jnp.where(mine, shard, jnp.zeros_like(shard)), axis)  286 us
    another operation x23, other arithmetic, per_device(): parent_pivot = jnp.linalg.cholesky(received[0])  124 us
    another operation x6, other arithmetic, solve_rows(): return jax.scipy.linalg.solve_triangular(factor, rows.T, lower=True).T  102 us
    another operation x14, other arithmetic, per_device(): pivot_factor = jnp.linalg.cholesky(whole_panel[:pivot_width])  89.1 us
    all_to_all x1, waiting for transfers between devices, per_device(): lax.all_to_all(outgoing_rows, 'leaf', split_axis=0, concat_axis=0, tiled=...  86 us
    all_to_all x1, waiting for transfers between devices, per_device(): lax.all_to_all(outgoing, 'col', split_axis=0, concat_axis=0, tiled=True)  48.2 us
    another operation x29, matrix products, solve_rows(): return jax.scipy.linalg.solve_triangular(factor, rows.T, lower=True).T  39.1 us
    all_gather x1, waiting for transfers between devices, per_device(): whole_panel = lax.all_gather(raw_panel, 'col', axis=0, tiled=True)  37 us
  transfers between devices with their start and end apart: 5, of which 5 were waited for; matrix products, arithmetic and copies ran while one was open for 1% of the time, Pallas kernels for 0%

commit v1 on v0

v1 whole, which is shorter than its diff:
```python
import functools

import jax
import jax.numpy as jnp
from jax import lax
from jax.experimental import pallas as pl
from jax.experimental.pallas import tpu as pltpu
from jax.sharding import PartitionSpec as P

B = 256
PC = 2
ROWBLK = 3
T = 128
W = 8

highest = lax.Precision.HIGHEST
high = lax.Precision.HIGH


def split3(x):
    h = x.astype(jnp.bfloat16)
    rest = x - h.astype(jnp.float32)
    m = rest.astype(jnp.bfloat16)
    l = (rest - m.astype(jnp.float32)).astype(jnp.bfloat16)
    return h.astype(jnp.float32), m.astype(jnp.float32), l.astype(jnp.float32)


def factor_tile(tile):
    rows = lax.broadcasted_iota(jnp.int32, (W, T), 0)
    lanes = lax.broadcasted_iota(jnp.int32, (W, T), 1)
    count = T // W
    a = [tile[W * p : W * p + W] for p in range(count)]
    v = [jnp.where(lanes == rows + W * p, 1.0, 0.0) for p in range(count)]
    for p in range(count):
        pa, pv = a[p], v[p]
        cb = [jnp.broadcast_to(pa[:, W * p + k : W * p + k + 1], (W, T)) for k in range(W)]
        for k in range(W):
            r = jnp.broadcast_to(lax.rsqrt(cb[k][k : k + 1]), (W, T))
            col = jnp.where(rows > k, cb[k] * r, 0.0)
            ra = jnp.broadcast_to(pa[k : k + 1], (W, T)) * r
            rv = jnp.broadcast_to(pv[k : k + 1], (W, T)) * r
            pa = jnp.where(rows == k, ra, pa - col * ra)
            pv = jnp.where(rows == k, rv, pv - col * rv)
            for k2 in range(k + 1, W):
                cb[k2] = cb[k2] - col * jnp.broadcast_to(col[k2 : k2 + 1], (W, T))
        a[p] = jnp.where(lanes >= rows + W * p, pa, 0.0)
        v[p] = pv
        if p < count - 1:
            both = jnp.concatenate([a[p], pv], 1)
            h, m, l = split3(both)
            left = jnp.concatenate([x[:, :T] for x in (h, h, m, h, l, m)], 0)
            right = jnp.concatenate([h, m, h, l, h, m], 0)
            delta = lax.dot_general(
                left.T.astype(jnp.bfloat16),
                right.astype(jnp.bfloat16),
                (((1,), (0,)), ((), ())),
                preferred_element_type=jnp.float32,
            )
            for q in range(p + 1, count):
                a[q] = a[q] - delta[W * q : W * q + W, :T]
                v[q] = v[q] - delta[W * q : W * q + W, T:]
    return jnp.concatenate(a, 0), jnp.concatenate(v, 0)


def mm(x, y):
    return jnp.dot(x, y, precision=highest, preferred_element_type=jnp.float32)


def mmt(x, y):
    return lax.dot_general(
        x, y, (((1,), (1,)), ((), ())), precision=highest, preferred_element_type=jnp.float32
    )


def chol_kernel(a_ref, l_ref, x_ref, work):
    n = a_ref.shape[0]
    count = n // T
    work[...] = a_ref[...]
    l_ref[...] = jnp.zeros_like(l_ref)
    x_ref[...] = jnp.zeros_like(x_ref)

    def step(j, carry):
        at = pl.ds(pl.multiple_of(j * T, T), T)
        upper, inverse = factor_tile(work[at, at])
        l_ref[at, at] = upper.T
        x_ref[at, at] = inverse
        for t in range(count):
            here = slice(t * T, t * T + T)

            @pl.when(j == t)
            def _():
                inv = x_ref[here, here]
                if t < count - 1:
                    below = slice(t * T + T, n)
                    panel = mmt(work[below, here], inv)
                    l_ref[below, here] = panel
                    for s in range(t + 1, count):
                        cut = slice(s * T, s * T + T)
                        work[s * T :, cut] = work[s * T :, cut] - mmt(
                            panel[(s - t - 1) * T :], panel[(s - t - 1) * T : (s - t) * T]
                        )
                if t > 0:
                    x_ref[here, : t * T] = -mm(inv, mm(l_ref[here, : t * T], x_ref[: t * T, : t * T]))

        return carry

    lax.fori_loop(0, count, step, 0)


def chol_inv(a):
    n = a.shape[0]
    shape = jax.ShapeDtypeStruct((n, n), jnp.float32)
    return pl.pallas_call(
        chol_kernel,
        out_shape=(shape, shape),
        in_specs=[pl.BlockSpec(memory_space=pltpu.VMEM)],
        out_specs=(pl.BlockSpec(memory_space=pltpu.VMEM),) * 2,
        scratch_shapes=[pltpu.VMEM((n, n), jnp.float32)],
        compiler_params=pltpu.CompilerParams(vmem_limit_bytes=32 * 2**20),
        cost_estimate=pl.CostEstimate(
            flops=n * 100_000_000, bytes_accessed=n * 300_000, transcendentals=n * 8
        ),
    )(a)


def place_kernel(child_count, slots, row_ref, col_ref, base_ref, piece_ref, out_ref):
    here = pl.program_id(0)
    out_ref[...] = base_ref[...]

    def body(k, carry):
        @pl.when(row_ref[k] == here)
        def _():
            for s in range(slots):
                q = col_ref[k * slots + s]

                @pl.when(q >= 0)
                def _():
                    at = pl.ds(pl.multiple_of(q * B, B), B)
                    out_ref[:, at] = out_ref[:, at] + piece_ref[k, :, s * B : s * B + B]

        return carry

    lax.fori_loop(0, child_count, body, 0)


def place(base, pieces, row_at, col_at):
    children, slots = col_at.shape
    rows, cols = base.shape
    return pl.pallas_call(
        functools.partial(place_kernel, children, slots),
        grid_spec=pltpu.PrefetchScalarGridSpec(
            num_scalar_prefetch=2,
            grid=(rows // B,),
            in_specs=[
                pl.BlockSpec((B, cols), lambda i, *_: (i, 0)),
                pl.BlockSpec(memory_space=pltpu.VMEM),
            ],
            out_specs=pl.BlockSpec((B, cols), lambda i, *_: (i, 0)),
        ),
        out_shape=jax.ShapeDtypeStruct(base.shape, jnp.float32),
        compiler_params=pltpu.CompilerParams(vmem_limit_bytes=48 * 2**20),
    )(row_at.astype(jnp.int32), col_at.reshape(-1).astype(jnp.int32), base, pieces)


def dot(x, y):
    return jnp.dot(x, y, precision=high, preferred_element_type=jnp.float32)


def find(mask):
    where = jnp.sum(
        jnp.where(mask, lax.broadcasted_iota(jnp.int32, mask.shape, mask.ndim - 1), 0), -1
    )
    return where, jnp.any(mask, -1)


def pick(array, index, size, axis, valid):
    block = lax.dynamic_slice_in_dim(array, index * size, size, axis)
    return jnp.where(valid, block, 0.0)


def route_slots(indices, col_blocks):
    target = indices // col_blocks
    count = indices.shape[-1]
    earlier_mask = lax.broadcasted_iota(jnp.int32, (count, count), 1) < lax.broadcasted_iota(
        jnp.int32, (count, count), 0
    )
    same = target[..., :, None] == target[..., None, :]
    ranking = jnp.sum((same & earlier_mask).astype(jnp.int32), axis=-1)
    return (target, ranking)


def per_device(child_fronts, child_index, parent_front):
    leaf_pos = lax.axis_index("leaf")
    col_pos = lax.axis_index("col")
    leaf_count = lax.axis_size("leaf")
    col_count = lax.axis_size("col")
    share = leaf_count // col_count
    children, contrib = child_index.shape
    front = child_fronts[0]
    row_count = front.shape[0]
    width = PC * B
    pivots = ROWBLK * B
    col_blocks = ROWBLK * leaf_count // col_count

    target, ranking = route_slots(child_index, col_blocks)
    own_index = lax.dynamic_index_in_dim(child_index, leaf_pos, 0, keepdims=False)
    own_target = lax.dynamic_index_in_dim(target, leaf_pos, 0, keepdims=False)
    own_rank = lax.dynamic_index_in_dim(ranking, leaf_pos, 0, keepdims=False)
    own_slot = own_target * share + own_rank
    slot_block, slot_valid = find(jnp.arange(col_count * share)[:, None] == own_slot[None])
    leaf_block, leaf_valid = find(jnp.arange(leaf_count)[:, None] == (own_index // ROWBLK)[None])
    zero_block, zero_valid = leaf_block[0], leaf_valid[0]

    panel = lax.all_gather(front[:, :width], "col", axis=0, tiled=True)
    trailing = front[:, width:]
    pivot_cols = lax.all_gather(
        pick(trailing, zero_block, B, 1, zero_valid), "col", axis=0, tiled=True
    )
    outgoing = jnp.concatenate(
        [pick(trailing, slot_block[i], B, 1, slot_valid[i])[None] for i in range(col_count * share)],
        0,
    ).reshape(col_count, share, row_count, B)
    raw_cols = lax.all_to_all(outgoing, "col", split_axis=0, concat_axis=0, tiled=True)

    first_leaf, first_col = leaf_pos == 0, col_pos == 0
    root = first_leaf & first_col
    corner = parent_front[:, :pivots]
    base_pivot = lax.psum(jnp.where(root, corner, 0.0), ("leaf", "col"))
    base_rows = lax.psum(jnp.where(first_col, corner, 0.0), "col")
    base_cols = lax.psum(jnp.where(first_leaf, parent_front, 0.0), "leaf")

    factor, inverse = chol_inv(panel[:width])
    solved = dot(panel, inverse.T)
    own_rows = lax.dynamic_slice_in_dim(solved, col_pos * row_count, row_count, 0)
    child_out = jnp.where(first_col, factor, own_rows)[None]
    below = solved[width:]

    first_slot = col_pos * share
    chosen = []
    for s in range(share):
        chosen.append(
            pick(
                below,
                lax.dynamic_index_in_dim(slot_block, first_slot + s, 0, keepdims=False),
                B,
                0,
                lax.dynamic_index_in_dim(slot_valid, first_slot + s, 0, keepdims=False),
            )
        )
    zero_rows = pick(below, zero_block, B, 0, zero_valid)

    pivot_schur = pivot_cols[width:] - dot(below, zero_rows.T)
    middle = pick(pivot_schur, zero_block, B, 0, zero_valid)
    diagonal = lax.all_gather(middle, "leaf", axis=0, tiled=False)

    crossing = jnp.concatenate(
        [
            pick(
                pivot_schur,
                lax.dynamic_index_in_dim(slot_block, first_slot + s, 0, keepdims=False),
                B,
                0,
                lax.dynamic_index_in_dim(slot_valid, first_slot + s, 0, keepdims=False),
            ).T
            for s in range(share)
        ],
        1,
    )
    crossing = lax.all_gather(crossing, "leaf", axis=0, tiled=False)

    raw = raw_cols.transpose(0, 2, 1, 3).reshape(col_count * row_count, share * B)[width:]
    schur_cols = raw - dot(below, jnp.concatenate(chosen, 0).T)
    sent = jnp.concatenate([schur_cols, pivot_schur], 1)
    outgoing_rows = jnp.concatenate(
        [pick(sent, leaf_block[i], B, 0, leaf_valid[i])[None] for i in range(leaf_count)], 0
    )
    arrived = lax.all_to_all(outgoing_rows, "leaf", split_axis=0, concat_axis=0, tiled=True)

    in_zero = child_index // ROWBLK == 0
    zero_any = jnp.any(in_zero, -1)
    zero_at = jnp.where(zero_any, jnp.sum(jnp.where(in_zero, child_index % ROWBLK, 0), -1), -1)
    parts = []
    for i in range(ROWBLK):
        here = base_pivot[i * B : i * B + B]
        added = jnp.sum(jnp.where((zero_at == i)[:, None, None], diagonal, 0.0), 0)
        parts.append(
            jnp.concatenate(
                [
                    here[:, j * B : j * B + B] + (added if i == j else 0.0)
                    for j in range(ROWBLK)
                ],
                1,
            )
        )
    parent_pivot, parent_inverse = chol_inv(jnp.concatenate(parts, 0))

    in_row = child_index // ROWBLK == leaf_pos
    row_block, row_valid = find(in_row)
    row_at = jnp.where(
        row_valid, jnp.sum(jnp.where(in_row, child_index % ROWBLK, 0), -1), -1
    )
    col_at = []
    for s in range(share):
        hit = (target == col_pos) & (ranking == s)
        col_at.append(
            jnp.where(
                jnp.any(hit, -1),
                jnp.sum(jnp.where(hit, child_index - col_pos * col_blocks, 0), -1),
                -1,
            )
        )
    col_at = jnp.stack(col_at, 1)

    own_cols = col_blocks
    joined = jnp.concatenate([parent_front, base_rows], 1)
    joined_at = jnp.concatenate(
        [col_at, jnp.where(zero_at >= 0, zero_at + own_cols, -1)[:, None]], 1
    )
    joined = place(joined, arrived, row_at, joined_at)
    assembled, raw_rows = joined[:, : own_cols * B], joined[:, own_cols * B :]
    raw_top = place(base_cols, crossing, zero_at, col_at)
    row_panel = dot(raw_rows, parent_inverse.T)
    top = dot(parent_inverse, raw_top)
    schur = assembled - dot(row_panel, top)
    left = jnp.where(first_leaf, parent_pivot, row_panel)
    right = jnp.where(first_leaf, 0.0, schur[:, pivots:])
    left = jnp.where(first_col, left, jnp.where(first_leaf, 0.0, schur[:, :pivots]))
    return (child_out, jnp.concatenate([left, right], 1))


def solution(mesh):
    placed = (P("leaf", "col", None), P(), P("leaf", "col"))
    return jax.shard_map(
        per_device,
        mesh=mesh,
        in_specs=placed,
        out_specs=(P("leaf", "col", None), P("leaf", "col")),
        check_vma=False,
    )
```

time: 1070 us -> 596 us (0.56)
  other arithmetic: 332 us -> 57.7 us
  waiting for transfers between devices: 457 us -> 330 us
  Pallas kernels: 0 us -> 87.3 us
  matrix products: 122 us -> 37.2 us
  local copies, waits for them, and re-layouts: 112 us -> 35.8 us
    another operation x43 -> x1, other arithmetic: 315 us -> 0.01 us  [per_device(): col_at = jnp.stack(col_at, 1)]
    pallas_call x0 -> x4, Pallas kernels: none -> 87.3 us  [the longest x2 70.7 us: chol_inv(): pl.pallas_call(chol_kernel, out_shape=(shape, shape), in_specs=[pl.BlockS...]
    all_to_all x1, waiting for transfers between devices: 86 us -> 0.01 us  [per_device(): lax.all_to_all(outgoing_rows, 'leaf', split_axis=0, concat_axis=0, tiled=...]
    another operation x45 -> x0, matrix products: 52.8 us -> none  [the longest x29 39.1 us: solve_rows(): return jax.scipy.linalg.solve_triangular(factor, rows.T, lower=True).T]
    another operation x70 -> x1, local copies, waits for them, and re-layouts: 37 us -> 0.08 us  [per_device(): col_at = jnp.stack(col_at, 1)]
    dot_general x6, matrix products: 69 us -> 37.2 us  [dot(): return jnp.dot(x, y, precision=high, preferred_element_type=jnp.float32)]
    unnamed x40 -> x30, local copies, waits for them, and re-layouts: 31.5 us -> 7.9 us
    reshape x4 -> x2, local copies, waits for them, and re-layouts: 22.2 us -> 0.16 us  [place(): col_at.reshape(-1).astype(jnp.int32)]
  transfers between devices with their start and end apart: 5 -> 9, of which waited for: 5 -> 5; matrix products, arithmetic and copies ran while one was open for 1% -> 17% of each run, Pallas kernels for 0% -> 13%
where the time goes in v1:
time: 596 us; the launch traced here: 586 us
  waiting for transfers between devices  330 us (55%)
  Pallas kernels  87.3 us (15%)
  other arithmetic  57.7 us (10%)
  matrix products  37.2 us (6%)
  local copies, waits for them, and re-layouts  35.8 us (6%)
  between operations  27.5 us (5%)
  starting transfers between devices  11.2 us (2%)
    psum x1, waiting for transfers between devices, per_device(): base_rows = lax.psum(jnp.where(first_col, corner, 0.0), 'col')  133 us
    psum x1, waiting for transfers between devices, per_device(): base_cols = lax.psum(jnp.where(first_leaf, parent_front, 0.0), 'leaf')  111 us
    pallas_call x2, Pallas kernels, chol_inv(): pl.pallas_call(chol_kernel, out_shape=(shape, shape), in_specs=[pl.BlockS...  70.7 us
    all_to_all x1, waiting for transfers between devices, per_device(): lax.all_to_all(outgoing, 'col', split_axis=0, concat_axis=0, tiled=True)  43.6 us
    dot_general x6, matrix products, dot(): return jnp.dot(x, y, precision=high, preferred_element_type=jnp.float32)  37.2 us
    all_gather x1, waiting for transfers between devices, per_device(): panel = lax.all_gather(front[:, :width], 'col', axis=0, tiled=True)  20.8 us
    psum x1, waiting for transfers between devices, per_device(): base_pivot = lax.psum(jnp.where(root, corner, 0.0), ('leaf', 'col'))  20.4 us
    unnamed x14, other arithmetic  20.3 us
  transfers between devices with their start and end apart: 9, of which 5 were waited for; matrix products, arithmetic and copies ran while one was open for 17% of the time, Pallas kernels for 13%

profile of v1, /device:TPU:0, one launch (start us, length us, event | category | flops | bytes accessed | tf_op | source)
XLA Modules:
  0.0 586.1 jit_solution(10833615075950514622)
XLA Ops:
  8.0 2.3 slice.222
  10.4 3.8 slice.225
  16.8 2.6 dynamic-slice_select_fusion.2
  19.5 4.4 slice_select_fusion.3
  27.6 20.8 %all-gather.7.cloned.1.call-done = f32[2048,512]{1,0:T(8,128)} async-done(((f32[512,512]{1,0:T(8,128)}), f32[2048,512]{1,0:T(8,128)}) %all-gather.7.cloned.1.call-update) | async-done | bytes 4194320 | tf_op jit(solution)/shard_map/all_gather | solution.py:214
  49.7 27.0 %shard_map.50 = (f32[512,512]{1,0:T(8,128)S(1)}, f32[512,512]{1,0:T(8,128)S(1)}) custom-call(f32[512,512]{1,0:T(8,128)S(1)} %slice.223.a_ref), custom_call_target="tpu_custom_call" | custom-call | flops 51200000000 | bytes 153600000 | tf_op jit(solution)/shard_map/pallas_call | solution.py:113
  76.7 3.7 fusion.62
  84.5 4.7 convolution_subtract_fusion.1
  89.2 2.7 select_bitcast_fusion.2
  110.0 4.9 all-to-all-start
  114.9 5.0 broadcast_select_fusion
  124.2 43.6 %all-to-all-done = f32[4,2,512,256]{3,2,1,0:T(8,128)} async-done(((f32[4,2,512,256]{3,2,1,0:T(8,128)}), f32[4,2,512,256]{3,2,1,0:T(8,128)}, u32[]{:S(2)}, u32[]{:S(2)}) %all-to-all-start) | async-done | bytes 4194336 | tf_op jit(solution)/shard_map/all_to_all | solution.py:223
  167.9 2.3 slice.234
  170.2 2.4 copy.38
  172.9 2.9 dynamic-slice_select_fusion.1
  175.8 2.8 convolution_subtract_fusion
  191.3 5.9 %all-to-all-start.1 = ((f32[8,256,768]{2,1,0:T(8,128)}), f32[8,256,768]{2,1,0:T(8,128)}, u32[]{:S(2)}, u32[]{:S(2)}) async-start(f32[8,256,768]{2,1,0:T(8,128)} %fusion.9), calls=%async_computation.1 | async-start | bytes 12582912 | tf_op jit(solution)/shard_map/all_to_all | solution.py:277
  197.6 20.4 %all-reduce.4.cloned.1.call-done = f32[768,768]{1,0:T(8,128)} async-done(((f32[768,768]{1,0:T(8,128)}), f32[768,768]{1,0:T(8,128)}) %all-reduce.4.cloned.1.call-update) | async-done | bytes 2359312 | tf_op jit(solution)/shard_map/psum | solution.py:228
  220.2 133.2 %all-reduce.6.cloned.1.call-done = f32[768,768]{1,0:T(8,128)} async-done(((f32[768,768]{1,0:T(8,128)}), f32[768,768]{1,0:T(8,128)}) %all-reduce.6.cloned.1.call-update) | async-done | bytes 2359312 | tf_op jit(solution)/shard_map/psum | solution.py:229
  353.4 6.4 %pad_maximum_fusion.base_ref = f32[768,2304]{1,0:T(8,128)} fusion(f32[768,768]{1,0:T(8,128)} %all-reduce.6.cloned.1.call-done, f32[768,1536]{1,0:T(8,128)} %param.5), kind=kLoop, calls=%fused_computation.16 | loop fusion | flops 1769472 | bytes 14155776 | tf_op jit(solution)/shard_map/concatenate | solution.py:315
  359.8 2.6 select_bitcast_fusion
  362.4 3.0 select_reduce_fusion.2
  365.8 43.7 %shard_map.51 = (f32[768,768]{1,0:T(8,128)S(1)}, f32[768,768]{1,0:T(8,128)S(1)}) custom-call(f32[768,768]{1,0:T(8,128)S(1)} %maximum_maximum_fusion.a_ref), custom_call_target="tpu_custom_call" | custom-call | flops 76800000000 | bytes 230400000 | tf_op jit(solution)/shard_map/pallas_call | solution.py:113
  410.9 5.4 copy.42
  416.2 110.9 %all-reduce.8.cloned.1.call-done.base_ref = f32[768,1536]{1,0:T(8,128)} async-done(((f32[768,1536]{1,0:T(8,128)}), f32[768,1536]{1,0:T(8,128)}) %all-reduce.8.cloned.1.call-update) | async-done | bytes 4718608 | tf_op jit(solution)/shard_map/psum | solution.py:230
  529.3 6.5 %shard_map.53 = f32[768,1536]{1,0:T(8,128)} custom-call(s32[8]{0:T(128)S(1)} %get-tuple-element.18.row_ref, s32[16]{0:T(128)S(1)} %reshape.132.col_ref, f32[768,1536]{1,0:T(8,128)} %all-reduce.8.cloned.1.call-done.base_ref, f32[8,256,512]{2,1,0:T(8,128)S(1)} %bitcast.114), custom_call_target="tpu_custom_call" | custom-call | tf_op jit(solution)/shard_map/pallas_call | solution.py:149
  535.8 9.4 %fusion.63 = f32[768,1536]{1,0:T(8,128)} fusion(f32[768,768]{1,0:T(8,128)S(1)} %copy-done.2, f32[768,1536]{1,0:T(8,128)} %shard_map.53), kind=kOutput, calls=%fused_computation.147 | convolution fusion | flops 5435817984 | bytes 11796480 | tf_op jit(solution)/shard_map/dot_general | solution.py:166
  545.3 10.1 %shard_map.52 = f32[768,2304]{1,0:T(8,128)} custom-call(s32[8]{0:T(128)S(1)} %broadcast_select_fusion.1.row_ref, s32[24]{0:T(128)S(1)} %reshape.130.col_ref, f32[768,2304]{1,0:T(8,128)} %pad_maximum_fusion.base_ref, f32[8,256,768]{2,1,0:T(8,128)} %all-to-all-done.1.piece_ref), custom_call_target="tpu_custom_call" | custom-call | tf_op jit(solution)/shard_map/pallas_call | solution.py:149
  555.3 6.0 %fusion.1 = f32[768,768]{0,1:T(8,128)} fusion(f32[768,768]{1,0:T(8,128)S(1)} %copy-done.3, f32[768,2304]{1,0:T(8,128)} %shard_map.52), kind=kOutput, calls=%fused_computation.24 | convolution fusion | flops 2717908992 | bytes 7077888 | tf_op jit(solution)/shard_map/dot_general | solution.py:166
  561.3 3.1 copy.40
  564.4 10.5 %slice_subtract_fusion = f32[768,1536]{1,0:T(8,128)S(1)} fusion(f32[768,2304]{1,0:T(8,128)} %shard_map.52, f32[768,768]{0,1:T(8,128)} %fusion.1, f32[768,1536]{1,0:T(8,128)} %fusion.63), kind=kOutput, calls=%fused_computation.17 | convolution fusion | flops 5436997632 | bytes 16515072 | tf_op jit(solution)/shard_map/dot_general | solution.py:166
  575.6 2.8 pad_maximum_fusion.1
  (101 shorter events, 43.2 us)
Async XLA Ops:
  8.0 40.4 %all-gather.7.cloned.1.call-start = ((), (), s32[]{:S(2)}) async-start(), calls=%async_computation.2 | async-start | bytes 5242880 | tf_op jit(solution)/shard_map/all_gather | solution.py:214
  10.3 3.8 copy-start.13
  10.3 74.2 %all-gather.9.cloned.1.call-start = ((), (), s32[]{:S(2)}) async-start(), calls=%async_computation.4 | async-start | bytes 2621440 | tf_op jit(solution)/shard_map/all_gather | solution.py:216
  19.4 198.6 %all-reduce.4.cloned.1.call-start = ((), (), s32[]{:S(2)}) async-start(), calls=%async_computation.3 | async-start | bytes 4718592 | tf_op jit(solution)/shard_map/psum | solution.py:228
  23.9 329.5 %all-reduce.6.cloned.1.call-start = ((), (), s32[]{:S(2)}) async-start(), calls=%async_computation.5 | async-start | bytes 4718592 | tf_op jit(solution)/shard_map/psum | solution.py:229
  24.5 337.9 %all-gather.11.cloned.1.call-start = ((), (), s32[]{:S(2)}) async-start(), calls=%async_computation.7 | async-start | bytes 2359296 | tf_op jit(solution)/shard_map/all_gather | solution.py:254
  49.7 27.0 %copy-start.8 = (f32[2048,512]{1,0:T(8,128)S(1)}, f32[2048,512]{1,0:T(8,128)}, u32[]{:S(2)}) copy-start(f32[2048,512]{1,0:T(8,128)} %all-gather.7.cloned.1.call-done) | copy-start | bytes 12582916
  80.5 1.9 copy-start.4
  91.9 318.9 %all-gather.13.cloned.1.call-start = ((), (), s32[]{:S(2)}) async-start(), calls=%async_computation.8 | async-start | bytes 4718592 | tf_op jit(solution)/shard_map/all_gather | solution.py:269
  98.0 7.3 %copy-start.6 = (f32[512,1536]{1,0:T(8,128)S(1)}, f32[512,1536]{1,0:T(8,128)}, u32[]{:S(2)}) copy-start(f32[512,1536]{1,0:T(8,128)} %slice.225) | copy-start | bytes 9437188
  108.0 2.0 copy-start.9
  110.0 57.8 %all-to-all-start = ((f32[4,2,512,256]{3,2,1,0:T(8,128)}), f32[4,2,512,256]{3,2,1,0:T(8,128)}, u32[]{:S(2)}, u32[]{:S(2)}) async-start(f32[4,2,512,256]{3,2,1,0:T(8,128)} %bitcast.117), calls=%async_computation | async-start | bytes 8388608 | tf_op jit(solution)/shard_map/all_to_all | solution.py:223
  114.9 412.2 %all-reduce.8.cloned.1.call-start = ((), (), s32[]{:S(2)}) async-start(), calls=%async_computation.6 | async-start | bytes 9437184 | tf_op jit(solution)/shard_map/psum | solution.py:230
  172.6 3.2 copy-start.5
  191.3 354.0 %all-to-all-start.1 = ((f32[8,256,768]{2,1,0:T(8,128)}), f32[8,256,768]{2,1,0:T(8,128)}, u32[]{:S(2)}, u32[]{:S(2)}) async-start(f32[8,256,768]{2,1,0:T(8,128)} %fusion.9), calls=%async_computation.1 | async-start | bytes 12582912 | tf_op jit(solution)/shard_map/all_to_all | solution.py:277
  359.8 5.6 copy-start.10
  362.4 3.2 copy-start.11
  362.4 3.2 copy-start.12
  409.5 1.4 copy-start.1
  527.1 2.2 copy-start
  529.3 6.5 %copy-start.2 = (f32[768,768]{1,0:T(8,128)S(1)}, f32[768,768]{1,0:T(8,128)}, u32[]{:S(2)}) copy-start(f32[768,768]{1,0:T(8,128)} %copy-done.1) | copy-start | bytes 7077892
  545.3 10.1 %copy-start.3 = (f32[768,768]{1,0:T(8,128)S(1)}, f32[768,768]{1,0:T(8,128)}, u32[]{:S(2)}) copy-start(f32[768,768]{1,0:T(8,128)} %copy-done.1) | copy-start | bytes 7077892
  564.4 10.6 %copy-start.7 = (f32[768,768]{1,0:T(8,128)S(1)}, f32[768,768]{1,0:T(8,128)}, u32[]{:S(2)}) copy-start(f32[768,768]{1,0:T(8,128)} %copy.40) | copy-start | bytes 7077892
Sparse Core Ops, SparseCore 0:
  11.0 37.3 all-gather.6
  50.0 22.6 all-gather.8
  92.0 49.7 all-gather.10
  143.9 121.0 all-gather.12
Sparse Core Ops, SparseCore 1:
  25.4 192.5 all-reduce.3
  220.3 133.0 all-reduce.5
  357.9 169.2 all-reduce.7

commit v2 on v1

--- a/solution.py
+++ b/solution.py
@@ -220,16 +220,25 @@
         [pick(trailing, slot_block[i], B, 1, slot_valid[i])[None] for i in range(col_count * share)],
         0,
     ).reshape(col_count, share, row_count, B)
+    first_leaf, first_col = leaf_pos == 0, col_pos == 0
+    corner = parent_front[:, :pivots]
+    part = pivots // col_count
+    quarter = jnp.where(first_col, corner[:part], 0.0)
+    for d in range(1, col_count):
+        quarter = quarter + lax.ppermute(corner[d * part : d * part + part], "col", [(0, d)])
+    quarter, panel, outgoing = lax.optimization_barrier((quarter, panel, outgoing))
+    quarter = lax.psum(jnp.where(first_leaf, quarter, 0.0), "leaf")
+    front_cols = jnp.where(first_leaf, parent_front, 0.0)
     raw_cols = lax.all_to_all(outgoing, "col", split_axis=0, concat_axis=0, tiled=True)
-
-    first_leaf, first_col = leaf_pos == 0, col_pos == 0
-    root = first_leaf & first_col
-    corner = parent_front[:, :pivots]
-    base_pivot = lax.psum(jnp.where(root, corner, 0.0), ("leaf", "col"))
-    base_rows = lax.psum(jnp.where(first_col, corner, 0.0), "col")
-    base_cols = lax.psum(jnp.where(first_leaf, parent_front, 0.0), "leaf")
-
     factor, inverse = chol_inv(panel[:width])
+    factor, inverse, raw_cols, corner, quarter, front_cols = lax.optimization_barrier(
+        (factor, inverse, raw_cols, corner, quarter, front_cols)
+    )
+    base_pivot = lax.all_gather(quarter, "col", axis=0, tiled=True)
+    base_cols = lax.psum(front_cols, "leaf")
+    base_rows = jnp.where(first_col, corner, 0.0)
+    for d in range(1, col_count):
+        base_rows = base_rows + lax.ppermute(corner, "col", [(0, d)])
     solved = dot(panel, inverse.T)
     own_rows = lax.dynamic_slice_in_dim(solved, col_pos * row_count, row_count, 0)
     child_out = jnp.where(first_col, factor, own_rows)[None]

time: 596 us -> 654 us (1.097)
  waiting for transfers between devices: 330 us -> 363 us
  starting transfers between devices: 11.2 us -> 29.8 us
    all_gather x1, waiting for transfers between devices: 0.01 us -> 93.2 us  [per_device(): crossing = lax.all_gather(crossing, 'leaf', axis=0, tiled=False)]
    psum x3 -> x2, waiting for transfers between devices: 264 us -> 202 us  [the longest x1 169 us: per_device(): base_cols = lax.psum(front_cols, 'leaf')]
    all_to_all x1, waiting for transfers between devices: 43.6 us -> 0.01 us  [per_device(): lax.all_to_all(outgoing, 'col', split_axis=0, concat_axis=0, tiled=True)]
    all_gather x1, waiting for transfers between devices: 0.01 us -> 32.6 us  [per_device(): diagonal = lax.all_gather(middle, 'leaf', axis=0, tiled=False)]
    ppermute x0 -> x6, waiting for transfers between devices: none -> 21.1 us  [the longest x3 15.1 us: per_device(): base_rows = base_rows + lax.ppermute(corner, 'col', [(0, d)])]
    all_gather x1, waiting for transfers between devices: 20.8 us -> 1.43 us  [per_device(): panel = lax.all_gather(front[:, :width], 'col', axis=0, tiled=True)]
    ppermute x0 -> x6, starting transfers between devices: none -> 18.3 us  [the longest x3 9.35 us: per_device(): lax.ppermute(corner[d * part:d * part + part], 'col', [(0, d)])]
    all_gather x1, waiting for transfers between devices: 0.01 us -> 12.6 us  [per_device(): lax.all_gather(pick(trailing, zero_block, B, 1, zero_valid), 'col', axis=...]
  transfers between devices with their start and end apart: 9 -> 15, of which waited for: 5 -> 8; matrix products, arithmetic and copies ran while one was open for 17% -> 16% of each run, Pallas kernels for 13% -> 12%
where the time goes in v2:
time: 654 us; the launch traced here: 644 us
  waiting for transfers between devices  363 us (56%)
  Pallas kernels  87.3 us (13%)
  other arithmetic  60.4 us (9%)
  matrix products  38.8 us (6%)
  local copies, waits for them, and re-layouts  38.6 us (6%)
  starting transfers between devices  29.8 us (5%)
  between operations  26.2 us (4%)
    psum x1, waiting for transfers between devices, per_device(): base_cols = lax.psum(front_cols, 'leaf')  169 us
    all_gather x1, waiting for transfers between devices, per_device(): crossing = lax.all_gather(crossing, 'leaf', axis=0, tiled=False)  93.2 us
    pallas_call x2, Pallas kernels, chol_inv(): pl.pallas_call(chol_kernel, out_shape=(shape, shape), in_specs=[pl.BlockS...  70.9 us
    dot_general x6, matrix products, dot(): return jnp.dot(x, y, precision=high, preferred_element_type=jnp.float32)  38.8 us
    psum x1, waiting for transfers between devices, per_device(): quarter = lax.psum(jnp.where(first_leaf, quarter, 0.0), 'leaf')  33.2 us
    all_gather x1, waiting for transfers between devices, per_device(): diagonal = lax.all_gather(middle, 'leaf', axis=0, tiled=False)  32.6 us
    unnamed x15, other arithmetic  21.9 us
    pallas_call x2, Pallas kernels, place(): pl.pallas_call(functools.partial(place_kernel, children, slots), grid_spe...  16.3 us
  transfers between devices with their start and end apart: 15, of which 8 were waited for; matrix products, arithmetic and copies ran while one was open for 16% of the time, Pallas kernels for 12%

profile of v2, /device:TPU:0, one launch (start us, length us, event | category | flops | bytes accessed | tf_op | source)
XLA Modules:
  0.0 644.4 jit_solution(15157098825717270373)
XLA Ops:
  12.2 5.1 collective-permute-start.2
  43.1 6.0 collective-permute-done.1
  58.8 3.2 slice.210
  62.0 5.0 broadcast_select_fusion
  68.3 5.4 all-to-all-start
  73.6 27.0 %shard_map.50 = (f32[512,512]{1,0:T(8,128)S(1)}, f32[512,512]{1,0:T(8,128)S(1)}) custom-call(f32[512,512]{1,0:T(8,128)S(1)} %slice.209.a_ref), custom_call_target="tpu_custom_call" | custom-call | flops 51200000000 | bytes 153600000 | tf_op jit(solution)/shard_map/pallas_call | solution.py:113
  100.6 33.2 %all-reduce.3.cloned.1.call-done = f32[192,768]{1,0:T(8,128)} async-done(((f32[192,768]{1,0:T(8,128)}), f32[192,768]{1,0:T(8,128)}) %all-reduce.3.cloned.1.call-update) | async-done | bytes 589840 | tf_op jit(solution)/shard_map/psum | solution.py:230
  135.1 5.3 fusion.63
  144.4 12.6 %all-gather.12.cloned.1.call-done = f32[2048,256]{1,0:T(8,128)} async-done(((f32[512,256]{1,0:T(8,128)}), f32[2048,256]{1,0:T(8,128)}) %all-gather.12.cloned.1.call-update) | async-done | bytes 2097168 | tf_op jit(solution)/shard_map/all_gather | solution.py:216
  157.0 4.7 convolution_subtract_fusion.1
  162.9 3.1 select_bitcast_fusion.2
  172.6 3.5 collective-permute-start.5
  176.1 2.7 collective-permute-start.4
  178.8 2.7 collective-permute-start.3
  186.6 2.9 dynamic-slice_select_fusion.1
  189.5 2.8 convolution_subtract_fusion
  205.2 5.7 all-to-all-start.1
  214.3 15.1 %collective-permute-done.4 = f32[768,768]{1,0:T(8,128)} collective-permute-done((f32[768,768]{1,0:T(8,128)S(1)}, f32[768,768]{1,0:T(8,128)}, u32[]{:S(2)}, u32[]{:S(2)}) %collective-permute-start.4) | collective-permute-done | bytes 2359328 | tf_op jit(solution)/shard_map/ppermute | solution.py:241
  229.4 3.7 add_add_fusion
  233.2 3.4 pad_maximum_fusion.base_ref
  238.0 32.6 %all-gather.14.cloned.1.call-done = f32[2048,256]{1,0:T(8,128)} async-done(((f32[256,256]{1,0:T(8,128)}), f32[2048,256]{1,0:T(8,128)}) %all-gather.14.cloned.1.call-update) | async-done | bytes 2097168 | tf_op jit(solution)/shard_map/all_gather | solution.py:263
  273.2 43.9 %shard_map.51 = (f32[768,768]{1,0:T(8,128)S(1)}, f32[768,768]{1,0:T(8,128)S(1)}) custom-call(f32[768,768]{1,0:T(8,128)S(1)} %maximum_maximum_fusion.a_ref), custom_call_target="tpu_custom_call" | custom-call | flops 76800000000 | bytes 230400000 | tf_op jit(solution)/shard_map/pallas_call | solution.py:113
  318.5 93.2 %all-gather.16.cloned.1.call-done = f32[2048,512]{0,1:T(8,128)} async-done(((f32[256,512]{0,1:T(8,128)}), f32[2048,512]{0,1:T(8,128)}) %all-gather.16.cloned.1.call-update) | async-done | bytes 4194320 | tf_op jit(solution)/shard_map/all_gather | solution.py:278
  411.7 5.4 copy.42
  417.1 169.0 %all-reduce.5.cloned.1.call-done.base_ref = f32[768,1536]{1,0:T(8,128)} async-done(((f32[768,1536]{1,0:T(8,128)}), f32[768,1536]{1,0:T(8,128)}) %all-reduce.5.cloned.1.call-update) | async-done | bytes 4718608 | tf_op jit(solution)/shard_map/psum | solution.py:238
  588.2 6.4 %shard_map.53 = f32[768,1536]{1,0:T(8,128)} custom-call(s32[8]{0:T(128)S(1)} %get-tuple-element.41.row_ref, s32[16]{0:T(128)S(1)} %reshape.132.col_ref, f32[768,1536]{1,0:T(8,128)} %all-reduce.5.cloned.1.call-done.base_ref, f32[8,256,512]{2,1,0:T(8,128)S(1)} %bitcast.114), custom_call_target="tpu_custom_call" | custom-call | tf_op jit(solution)/shard_map/pallas_call | solution.py:149
  594.7 9.4 %fusion.64 = f32[768,1536]{1,0:T(8,128)} fusion(f32[768,768]{1,0:T(8,128)S(1)} %copy-done.2, f32[768,1536]{1,0:T(8,128)} %shard_map.53), kind=kOutput, calls=%fused_computation.149 | convolution fusion | flops 5435817984 | bytes 11796480 | tf_op jit(solution)/shard_map/dot_general | solution.py:166
  604.1 9.9 %shard_map.52 = f32[768,2304]{1,0:T(8,128)} custom-call(s32[8]{0:T(128)S(1)} %broadcast_select_fusion.2.row_ref, s32[24]{0:T(128)S(1)} %reshape.131.col_ref, f32[768,2304]{1,0:T(8,128)} %pad_maximum_fusion.base_ref, f32[8,256,768]{2,1,0:T(8,128)} %all-to-all-done.1.piece_ref), custom_call_target="tpu_custom_call" | custom-call | tf_op jit(solution)/shard_map/pallas_call | solution.py:149
  614.0 6.0 fusion.1
  620.0 3.1 copy.40
  623.1 10.5 %slice_subtract_fusion = f32[768,1536]{1,0:T(8,128)S(1)} fusion(f32[768,2304]{1,0:T(8,128)} %shard_map.52, f32[768,768]{0,1:T(8,128)} %fusion.1, f32[768,1536]{1,0:T(8,128)} %fusion.64), kind=kOutput, calls=%fused_computation.17 | convolution fusion | flops 5436997632 | bytes 16515072 | tf_op jit(solution)/shard_map/dot_general | solution.py:166
  634.3 2.8 pad_maximum_fusion.1
  (117 shorter events, 73.0 us)
Async XLA Ops:
  7.2 45.8 %all-gather.8.cloned.1.call-start = ((), (), s32[]{:S(2)}) async-start(), calls=%async_computation.2 | async-start | bytes 5242880 | tf_op jit(solution)/shard_map/all_gather | solution.py:214
  9.5 124.3 %all-reduce.3.cloned.1.call-start = ((), (), s32[]{:S(2)}) async-start(), calls=%async_computation.3 | async-start | bytes 1179648 | tf_op jit(solution)/shard_map/psum | solution.py:230
  12.2 30.8 %collective-permute-start.2 = (f32[192,768]{1,0:T(8,128)}, f32[192,768]{1,0:T(8,128)}, u32[]{:S(2)}, u32[]{:S(2)}) collective-permute-start(f32[192,768]{1,0:T(8,128)} %get-tuple-element.48), channel_id=1, source_target_pairs={{0,3},{4,7},{8,11},{12,15},{16,19},{20,23},{24,27},{28,31}} | collective-permute-start | bytes 1769480 | tf_op jit(solution)/shard_map/ppermute | solution.py:228
  17.4 31.7 %collective-permute-start.1 = (f32[192,768]{1,0:T(8,128)}, f32[192,768]{1,0:T(8,128)}, u32[]{:S(2)}, u32[]{:S(2)}) collective-permute-start(f32[192,768]{1,0:T(8,128)} %get-tuple-element.49), channel_id=1, source_target_pairs={{0,2},{4,6},{8,10},{12,14},{16,18},{20,22},{24,26},{28,30}} | collective-permute-start | bytes 1769480 | tf_op jit(solution)/shard_map/ppermute | solution.py:228
  19.5 29.6 %collective-permute-start = (f32[192,768]{1,0:T(8,128)}, f32[192,768]{1,0:T(8,128)}, u32[]{:S(2)}, u32[]{:S(2)}) collective-permute-start(f32[192,768]{1,0:T(8,128)} %get-tuple-element.47), channel_id=1, source_target_pairs={{0,1},{4,5},{8,9},{12,13},{16,17},{20,21},{24,25},{28,29}} | collective-permute-start | bytes 1769480 | tf_op jit(solution)/shard_map/ppermute | solution.py:228
  21.6 2.3 copy-start.11
  55.0 102.0 %all-gather.12.cloned.1.call-start = ((), (), s32[]{:S(2)}) async-start(), calls=%async_computation.5 | async-start | bytes 2621440 | tf_op jit(solution)/shard_map/all_gather | solution.py:216
  68.3 65.5 %all-to-all-start = ((f32[4,2,512,256]{3,2,1,0:T(8,128)}), f32[4,2,512,256]{3,2,1,0:T(8,128)}, u32[]{:S(2)}, u32[]{:S(2)}) async-start(f32[4,2,512,256]{3,2,1,0:T(8,128)} %bitcast.25), calls=%async_computation | async-start | bytes 8388608 | tf_op jit(solution)/shard_map/all_to_all | solution.py:232
  73.6 162.9 %all-gather.10.cloned.1.call-start = ((), (), s32[]{:S(2)}) async-start(), calls=%async_computation.4 | async-start | bytes 2949120 | tf_op jit(solution)/shard_map/all_gather | solution.py:237
  133.8 136.8 %all-gather.14.cloned.1.call-start = ((), (), s32[]{:S(2)}) async-start(), calls=%async_computation.7 | async-start | bytes 2359296 | tf_op jit(solution)/shard_map/all_gather | solution.py:263
  140.5 1.9 copy-start.6
  161.7 1.2 copy-start.4
  161.7 10.9 %copy-start.9 = (f32[768,768]{1,0:T(8,128)S(1)}, f32[768,768]{1,0:T(8,128)}, u32[]{:S(2)}) copy-start(f32[768,768]{1,0:T(8,128)} %slice.210) | copy-start | bytes 7077892
  166.0 245.8 %all-gather.16.cloned.1.call-start = ((), (), s32[]{:S(2)}) async-start(), calls=%async_computation.8 | async-start | bytes 4718592 | tf_op jit(solution)/shard_map/all_gather | solution.py:278
  172.6 41.7 %collective-permute-start.5 = (f32[768,768]{1,0:T(8,128)S(1)}, f32[768,768]{1,0:T(8,128)}, u32[]{:S(2)}, u32[]{:S(2)}) collective-permute-start(f32[768,768]{1,0:T(8,128)S(1)} %copy-done.9), channel_id=1, source_target_pairs={{0,3},{4,7},{8,11},{12,15},{16,19},{20,23},{24,27},{28,31}} | collective-permute-start | bytes 7077896 | tf_op jit(solution)/shard_map/ppermute | solution.py:241
  176.1 53.3 %collective-permute-start.4 = (f32[768,768]{1,0:T(8,128)S(1)}, f32[768,768]{1,0:T(8,128)}, u32[]{:S(2)}, u32[]{:S(2)}) collective-permute-start(f32[768,768]{1,0:T(8,128)S(1)} %copy-done.9), channel_id=1, source_target_pairs={{0,2},{4,6},{8,10},{12,14},{16,18},{20,22},{24,26},{28,30}} | collective-permute-start | bytes 7077896 | tf_op jit(solution)/shard_map/ppermute | solution.py:241
  178.8 50.7 %collective-permute-start.3 = (f32[768,768]{1,0:T(8,128)S(1)}, f32[768,768]{1,0:T(8,128)}, u32[]{:S(2)}, u32[]{:S(2)}) collective-permute-start(f32[768,768]{1,0:T(8,128)S(1)} %copy-done.9), channel_id=1, source_target_pairs={{0,1},{4,5},{8,9},{12,13},{16,17},{20,21},{24,25},{28,29}} | collective-permute-start | bytes 7077896 | tf_op jit(solution)/shard_map/ppermute | solution.py:241
  186.2 3.3 copy-start.7
  189.5 2.8 copy-start.5
  205.2 398.9 %all-to-all-start.1 = ((f32[8,256,768]{2,1,0:T(8,128)}), f32[8,256,768]{2,1,0:T(8,128)}, u32[]{:S(2)}, u32[]{:S(2)}) async-start(f32[8,256,768]{2,1,0:T(8,128)} %fusion.9), calls=%async_computation.1 | async-start | bytes 12582912 | tf_op jit(solution)/shard_map/all_to_all | solution.py:286
  211.0 375.1 %all-reduce.5.cloned.1.call-start = ((), (), s32[]{:S(2)}) async-start(), calls=%async_computation.6 | async-start | bytes 9437184 | tf_op jit(solution)/shard_map/psum | solution.py:238
  211.7 21.4 %slice-start = ((s8[4718592]{0:T(1024)(128)(4,1)}), s8[4194304]{0:T(1024)(128)(4,1)S(1)}, s32[]{:S(2)}) async-start(s8[4718592]{0:T(1024)(128)(4,1)} %bitcast.115), calls=%async_computation.9 | async-start | bytes 8388608
  214.3 18.8 %slice-start.1 = ((s8[4718592]{0:T(1024)(128)(4,1)}), s8[524288]{0:T(1024)(128)(4,1)S(1)}, s32[]{:S(2)}) async-start(s8[4718592]{0:T(1024)(128)(4,1)} %bitcast.115), calls=%async_computation.10 | async-start | bytes 1048576
  236.5 36.3 %copy-start.10 = (f32[768,768]{1,0:T(8,128)S(1)}, f32[768,768]{1,0:T(8,128)}, u32[]{:S(2)}) copy-start(f32[768,768]{1,0:T(8,128)} %all-gather.10.cloned.1.call-done) | copy-start | bytes 7077892
  317.1 1.4 copy-start.1
  586.0 2.2 copy-start
  588.2 6.5 %copy-start.2 = (f32[768,768]{1,0:T(8,128)S(1)}, f32[768,768]{1,0:T(8,128)}, u32[]{:S(2)}) copy-start(f32[768,768]{1,0:T(8,128)} %copy-done.1) | copy-start | bytes 7077892
  604.1 9.9 %copy-start.3 = (f32[768,768]{1,0:T(8,128)S(1)}, f32[768,768]{1,0:T(8,128)}, u32[]{:S(2)}) copy-start(f32[768,768]{1,0:T(8,128)} %copy-done.1) | copy-start | bytes 7077892
  623.1 10.6 %copy-start.8 = (f32[768,768]{1,0:T(8,128)S(1)}, f32[768,768]{1,0:T(8,128)}, u32[]{:S(2)}) copy-start(f32[768,768]{1,0:T(8,128)} %copy.40) | copy-start | bytes 7077892
Sparse Core Ops, SparseCore 0:
  10.1 42.8 all-gather.7
  57.0 76.7 all-reduce.2
  135.4 21.4 all-gather.11
  158.5 26.1 all-gather.9
  186.9 83.6 all-gather.13
  272.7 138.9 all-gather.15
  416.3 169.6 all-reduce.4

commit v3 on v2

--- a/solution.py
+++ b/solution.py
@@ -227,15 +227,14 @@
     for d in range(1, col_count):
         quarter = quarter + lax.ppermute(corner[d * part : d * part + part], "col", [(0, d)])
     quarter, panel, outgoing = lax.optimization_barrier((quarter, panel, outgoing))
-    quarter = lax.psum(jnp.where(first_leaf, quarter, 0.0), "leaf")
     front_cols = jnp.where(first_leaf, parent_front, 0.0)
     raw_cols = lax.all_to_all(outgoing, "col", split_axis=0, concat_axis=0, tiled=True)
     factor, inverse = chol_inv(panel[:width])
     factor, inverse, raw_cols, corner, quarter, front_cols = lax.optimization_barrier(
         (factor, inverse, raw_cols, corner, quarter, front_cols)
     )
+    quarter = lax.psum(jnp.where(first_leaf, quarter, 0.0), "leaf")
     base_pivot = lax.all_gather(quarter, "col", axis=0, tiled=True)
-    base_cols = lax.psum(front_cols, "leaf")
     base_rows = jnp.where(first_col, corner, 0.0)
     for d in range(1, col_count):
         base_rows = base_rows + lax.ppermute(corner, "col", [(0, d)])
@@ -275,7 +274,29 @@
         ],
         1,
     )
-    crossing = lax.all_gather(crossing, "leaf", axis=0, tiled=False)
+    in_zero = child_index // ROWBLK == 0
+    zero_any = jnp.any(in_zero, -1)
+    zero_at = jnp.where(zero_any, jnp.sum(jnp.where(in_zero, child_index % ROWBLK, 0), -1), -1)
+    col_at = []
+    for s in range(share):
+        hit = (target == col_pos) & (ranking == s)
+        col_at.append(
+            jnp.where(
+                jnp.any(hit, -1),
+                jnp.sum(jnp.where(hit, child_index - col_pos * col_blocks, 0), -1),
+                -1,
+            )
+        )
+    col_at = jnp.stack(col_at, 1)
+
+    raw_top = place(
+        front_cols,
+        crossing[None],
+        lax.dynamic_slice_in_dim(zero_at, leaf_pos, 1, 0),
+        lax.dynamic_slice_in_dim(col_at, leaf_pos, 1, 0),
+    )
+    raw_top, base_pivot = lax.optimization_barrier((raw_top, base_pivot))
+    raw_top = lax.psum(raw_top, "leaf")
 
     raw = raw_cols.transpose(0, 2, 1, 3).reshape(col_count * row_count, share * B)[width:]
     schur_cols = raw - dot(below, jnp.concatenate(chosen, 0).T)
@@ -285,9 +306,6 @@
     )
     arrived = lax.all_to_all(outgoing_rows, "leaf", split_axis=0, concat_axis=0, tiled=True)
 
-    in_zero = child_index // ROWBLK == 0
-    zero_any = jnp.any(in_zero, -1)
-    zero_at = jnp.where(zero_any, jnp.sum(jnp.where(in_zero, child_index % ROWBLK, 0), -1), -1)
     parts = []
     for i in range(ROWBLK):
         here = base_pivot[i * B : i * B + B]
@@ -308,18 +326,6 @@
     row_at = jnp.where(
         row_valid, jnp.sum(jnp.where(in_row, child_index % ROWBLK, 0), -1), -1
     )
-    col_at = []
-    for s in range(share):
-        hit = (target == col_pos) & (ranking == s)
-        col_at.append(
-            jnp.where(
-                jnp.any(hit, -1),
-                jnp.sum(jnp.where(hit, child_index - col_pos * col_blocks, 0), -1),
-                -1,
-            )
-        )
-    col_at = jnp.stack(col_at, 1)
-
     own_cols = col_blocks
     joined = jnp.concatenate([parent_front, base_rows], 1)
     joined_at = jnp.concatenate(
@@ -327,7 +333,6 @@
     )
     joined = place(joined, arrived, row_at, joined_at)
     assembled, raw_rows = joined[:, : own_cols * B], joined[:, own_cols * B :]
-    raw_top = place(base_cols, crossing, zero_at, col_at)
     row_panel = dot(raw_rows, parent_inverse.T)
     top = dot(parent_inverse, raw_top)
     schur = assembled - dot(row_panel, top)

time: 654 us -> 596 us (0.911)
  waiting for transfers between devices: 363 us -> 313 us
    all_gather x1 -> x0, waiting for transfers between devices: 93.2 us -> none  [per_device(): crossing = lax.all_gather(crossing, 'leaf', axis=0, tiled=False)]
    all_gather x1, waiting for transfers between devices: 32.6 us -> 107 us  [per_device(): diagonal = lax.all_gather(middle, 'leaf', axis=0, tiled=False)]
    psum x1, waiting for transfers between devices: 169 us -> 127 us  [per_device(): raw_top = lax.psum(raw_top, 'leaf')]
    all_to_all x1, waiting for transfers between devices: 0.01 us -> 32.3 us  [per_device(): lax.all_to_all(outgoing, 'col', split_axis=0, concat_axis=0, tiled=True)]
    all_gather x1, waiting for transfers between devices: 0.01 us -> 20.6 us  [per_device(): base_pivot = lax.all_gather(quarter, 'col', axis=0, tiled=True)]
    ppermute x3, waiting for transfers between devices: 15.1 us -> 0.01 us  [per_device(): base_rows = base_rows + lax.ppermute(corner, 'col', [(0, d)])]
    all_gather x1, waiting for transfers between devices: 12.6 us -> 0.01 us  [per_device(): lax.all_gather(pick(trailing, zero_block, B, 1, zero_valid), 'col', axis=...]
    psum x1, waiting for transfers between devices: 33.2 us -> 26 us  [per_device(): quarter = lax.psum(jnp.where(first_leaf, quarter, 0.0), 'leaf')]
  transfers between devices with their start and end apart: 15 -> 14, of which waited for: 8 -> 5; matrix products, arithmetic and copies ran while one was open for 16% -> 17% of each run, Pallas kernels for 12% -> 13%
where the time goes in v3:
time: 596 us; the launch traced here: 587 us
  waiting for transfers between devices  313 us (53%)
  Pallas kernels  85.2 us (14%)
  other arithmetic  59.3 us (10%)
  matrix products  39.5 us (7%)
  local copies, waits for them, and re-layouts  34.8 us (6%)
  starting transfers between devices  28.3 us (5%)
  between operations  26.2 us (4%)
    psum x1, waiting for transfers between devices, per_device(): raw_top = lax.psum(raw_top, 'leaf')  127 us
    all_gather x1, waiting for transfers between devices, per_device(): diagonal = lax.all_gather(middle, 'leaf', axis=0, tiled=False)  107 us
    pallas_call x2, Pallas kernels, chol_inv(): pl.pallas_call(chol_kernel, out_shape=(shape, shape), in_specs=[pl.BlockS...  70.7 us
    dot_general x6, matrix products, dot(): return jnp.dot(x, y, precision=high, preferred_element_type=jnp.float32)  39.5 us
    all_to_all x1, waiting for transfers between devices, per_device(): lax.all_to_all(outgoing, 'col', split_axis=0, concat_axis=0, tiled=True)  32.3 us
    psum x1, waiting for transfers between devices, per_device(): quarter = lax.psum(jnp.where(first_leaf, quarter, 0.0), 'leaf')  26 us
    unnamed x15, other arithmetic  22.8 us
    all_gather x1, waiting for transfers between devices, per_device(): base_pivot = lax.all_gather(quarter, 'col', axis=0, tiled=True)  20.6 us
  transfers between devices with their start and end apart: 14, of which 5 were waited for; matrix products, arithmetic and copies ran while one was open for 17% of the time, Pallas kernels for 13%

profile of v3, /device:TPU:0, one launch (start us, length us, event | category | flops | bytes accessed | tf_op | source)
XLA Modules:
  0.0 586.6 jit_solution(9306329988112587940)
XLA Ops:
  9.5 2.7 fusion.58
  12.3 5.1 collective-permute-start.2
  34.2 3.2 slice.210
  51.3 5.0 broadcast_select_fusion.base_ref
  56.3 2.6 add_add_fusion.1
  60.2 4.9 all-to-all-start
  65.1 27.0 %shard_map.50 = (f32[512,512]{1,0:T(8,128)S(1)}, f32[512,512]{1,0:T(8,128)S(1)}) custom-call(f32[512,512]{1,0:T(8,128)S(1)} %slice.209.a_ref), custom_call_target="tpu_custom_call" | custom-call | flops 51200000000 | bytes 153600000 | tf_op jit(solution)/shard_map/pallas_call | solution.py:113
  92.1 32.3 %all-to-all-done = f32[4,2,512,256]{3,2,1,0:T(8,128)} async-done(((f32[4,2,512,256]{3,2,1,0:T(8,128)}), f32[4,2,512,256]{3,2,1,0:T(8,128)}, u32[]{:S(2)}, u32[]{:S(2)}) %all-to-all-start) | async-done | bytes 4194336 | tf_op jit(solution)/shard_map/all_to_all | solution.py:231
  126.5 5.3 fusion.64
  135.7 4.6 convolution_subtract_fusion.1
  140.3 2.6 select_bitcast_fusion.2
  147.7 3.4 collective-permute-start.5
  151.1 2.7 collective-permute-start.4
  153.8 2.8 collective-permute-start.3
  161.6 2.8 dynamic-slice_select_fusion.1
  164.4 2.8 convolution_subtract_fusion
  170.5 26.0 %all-reduce.3.cloned.1.call-done = f32[192,768]{1,0:T(8,128)} async-done(((f32[192,768]{1,0:T(8,128)}), f32[192,768]{1,0:T(8,128)}) %all-reduce.3.cloned.1.call-update) | async-done | bytes 589840 | tf_op jit(solution)/shard_map/psum | solution.py:236
  196.6 3.0 fusion.17
  209.0 4.7 all-to-all-start.1
  215.0 4.6 shard_map.51
  224.4 3.9 add_add_fusion
  228.4 3.4 pad_maximum_fusion.base_ref
  231.8 107.5 %all-gather.12.cloned.1.call-done = f32[2048,256]{1,0:T(8,128)} async-done(((f32[256,256]{1,0:T(8,128)}), f32[2048,256]{1,0:T(8,128)}) %all-gather.12.cloned.1.call-update) | async-done | bytes 2097168 | tf_op jit(solution)/shard_map/all_gather | solution.py:262
  341.5 20.6 %all-gather.10.cloned.1.call-done = f32[768,768]{1,0:T(8,128)} async-done(((f32[192,768]{1,0:T(8,128)}), f32[768,768]{1,0:T(8,128)}) %all-gather.10.cloned.1.call-update) | async-done | bytes 2359312 | tf_op jit(solution)/shard_map/all_gather | solution.py:237
  364.3 43.7 %shard_map.52 = (f32[768,768]{1,0:T(8,128)S(1)}, f32[768,768]{1,0:T(8,128)S(1)}) custom-call(f32[768,768]{1,0:T(8,128)S(1)} %maximum_maximum_fusion.a_ref), custom_call_target="tpu_custom_call" | custom-call | flops 76800000000 | bytes 230400000 | tf_op jit(solution)/shard_map/pallas_call | solution.py:113
  409.5 126.8 %all-reduce.5.cloned.1.call-done = f32[768,1536]{1,0:T(8,128)} async-done(((f32[768,1536]{1,0:T(8,128)}), f32[768,1536]{1,0:T(8,128)}) %all-reduce.5.cloned.1.call-update) | async-done | bytes 4718608 | tf_op jit(solution)/shard_map/psum | solution.py:299
  536.3 10.1 %fusion.65 = f32[768,1536]{1,0:T(8,128)} fusion(f32[768,768]{1,0:T(8,128)} %copy-done.1, f32[768,1536]{1,0:T(8,128)} %all-reduce.5.cloned.1.call-done), kind=kOutput, calls=%fused_computation.151 | convolution fusion | flops 5435817984 | bytes 11796480 | tf_op jit(solution)/shard_map/dot_general | solution.py:166
  546.4 9.9 %shard_map.53 = f32[768,2304]{1,0:T(8,128)} custom-call(s32[8]{0:T(128)S(1)} %broadcast_select_fusion.2.row_ref, s32[24]{0:T(128)S(1)} %reshape.132.col_ref, f32[768,2304]{1,0:T(8,128)} %pad_maximum_fusion.base_ref, f32[8,256,768]{2,1,0:T(8,128)} %all-to-all-done.1.piece_ref), custom_call_target="tpu_custom_call" | custom-call | tf_op jit(solution)/shard_map/pallas_call | solution.py:149
  556.2 6.1 %fusion.1 = f32[768,768]{0,1:T(8,128)} fusion(f32[768,768]{1,0:T(8,128)S(1)} %copy-done.2, f32[768,2304]{1,0:T(8,128)} %shard_map.53), kind=kOutput, calls=%fused_computation.24 | convolution fusion | flops 2717908992 | bytes 7077888 | tf_op jit(solution)/shard_map/dot_general | solution.py:166
  562.3 3.1 copy.38
  565.4 10.5 %slice_subtract_fusion = f32[768,1536]{1,0:T(8,128)S(1)} fusion(f32[768,2304]{1,0:T(8,128)} %shard_map.53, f32[768,768]{0,1:T(8,128)} %fusion.1, f32[768,1536]{1,0:T(8,128)} %fusion.65), kind=kOutput, calls=%fused_computation.17 | convolution fusion | flops 5436997632 | bytes 16515072 | tf_op jit(solution)/shard_map/dot_general | solution.py:166
  576.5 2.8 pad_maximum_fusion.1
  (112 shorter events, 63.9 us)
Async XLA Ops:
  7.2 51.7 %all-gather.6.cloned.1.call-start = ((), (), s32[]{:S(2)}) async-start(), calls=%async_computation.2 | async-start | bytes 5242880 | tf_op jit(solution)/shard_map/all_gather | solution.py:214
  9.5 126.2 %all-gather.8.cloned.1.call-start = ((), (), s32[]{:S(2)}) async-start(), calls=%async_computation.3 | async-start | bytes 2621440 | tf_op jit(solution)/shard_map/all_gather | solution.py:216
  12.3 44.0 %collective-permute-start.2 = (f32[192,768]{1,0:T(8,128)}, f32[192,768]{1,0:T(8,128)}, u32[]{:S(2)}, u32[]{:S(2)}) collective-permute-start(f32[192,768]{1,0:T(8,128)} %get-tuple-element.52), channel_id=1, source_target_pairs={{0,3},{4,7},{8,11},{12,15},{16,19},{20,23},{24,27},{28,31}} | collective-permute-start | bytes 1769480 | tf_op jit(solution)/shard_map/ppermute | solution.py:228
  17.4 38.9 %collective-permute-start.1 = (f32[192,768]{1,0:T(8,128)}, f32[192,768]{1,0:T(8,128)}, u32[]{:S(2)}, u32[]{:S(2)}) collective-permute-start(f32[192,768]{1,0:T(8,128)} %get-tuple-element.53), channel_id=1, source_target_pairs={{0,2},{4,6},{8,10},{12,14},{16,18},{20,22},{24,26},{28,30}} | collective-permute-start | bytes 1769480 | tf_op jit(solution)/shard_map/ppermute | solution.py:228
  19.5 36.8 %collective-permute-start = (f32[192,768]{1,0:T(8,128)}, f32[192,768]{1,0:T(8,128)}, u32[]{:S(2)}, u32[]{:S(2)}) collective-permute-start(f32[192,768]{1,0:T(8,128)} %get-tuple-element.51), channel_id=1, source_target_pairs={{0,1},{4,5},{8,9},{12,13},{16,17},{20,21},{24,25},{28,29}} | collective-permute-start | bytes 1769480 | tf_op jit(solution)/shard_map/ppermute | solution.py:228
  21.6 2.3 copy-start.10
  60.2 64.3 %all-to-all-start = ((f32[4,2,512,256]{3,2,1,0:T(8,128)}), f32[4,2,512,256]{3,2,1,0:T(8,128)}, u32[]{:S(2)}, u32[]{:S(2)}) async-start(f32[4,2,512,256]{3,2,1,0:T(8,128)} %bitcast.119), calls=%async_computation | async-start | bytes 8388608 | tf_op jit(solution)/shard_map/all_to_all | solution.py:231
  65.1 131.5 %all-reduce.3.cloned.1.call-start = ((), (), s32[]{:S(2)}) async-start(), calls=%async_computation.4 | async-start | bytes 1179648 | tf_op jit(solution)/shard_map/psum | solution.py:236
  126.4 212.8 %all-gather.12.cloned.1.call-start = ((), (), s32[]{:S(2)}) async-start(), calls=%async_computation.7 | async-start | bytes 2359296 | tf_op jit(solution)/shard_map/all_gather | solution.py:262
  131.8 1.9 copy-start.5
  142.9 219.2 %all-gather.10.cloned.1.call-start = ((), (), s32[]{:S(2)}) async-start(), calls=%async_computation.5 | async-start | bytes 2949120 | tf_op jit(solution)/shard_map/all_gather | solution.py:237
  147.7 76.7 %collective-permute-start.5 = (f32[768,768]{1,0:T(8,128)}, f32[768,768]{1,0:T(8,128)}, u32[]{:S(2)}, u32[]{:S(2)}) collective-permute-start(f32[768,768]{1,0:T(8,128)} %slice.210), channel_id=1, source_target_pairs={{0,3},{4,7},{8,11},{12,15},{16,19},{20,23},{24,27},{28,31}} | collective-permute-start | bytes 7077896 | tf_op jit(solution)/shard_map/ppermute | solution.py:240
  151.1 73.3 %collective-permute-start.4 = (f32[768,768]{1,0:T(8,128)}, f32[768,768]{1,0:T(8,128)}, u32[]{:S(2)}, u32[]{:S(2)}) collective-permute-start(f32[768,768]{1,0:T(8,128)} %slice.210), channel_id=1, source_target_pairs={{0,2},{4,6},{8,10},{12,14},{16,18},{20,22},{24,26},{28,30}} | collective-permute-start | bytes 7077896 | tf_op jit(solution)/shard_map/ppermute | solution.py:240
  153.8 70.6 %collective-permute-start.3 = (f32[768,768]{1,0:T(8,128)}, f32[768,768]{1,0:T(8,128)}, u32[]{:S(2)}, u32[]{:S(2)}) collective-permute-start(f32[768,768]{1,0:T(8,128)} %slice.210), channel_id=1, source_target_pairs={{0,1},{4,5},{8,9},{12,13},{16,17},{20,21},{24,25},{28,29}} | collective-permute-start | bytes 7077896 | tf_op jit(solution)/shard_map/ppermute | solution.py:240
  161.3 3.2 copy-start.6
  167.2 1.7 copy-start.3
  196.6 3.0 copy-start.4
  209.0 337.4 %all-to-all-start.1 = ((f32[8,256,768]{2,1,0:T(8,128)}), f32[8,256,768]{2,1,0:T(8,128)}, u32[]{:S(2)}, u32[]{:S(2)}) async-start(f32[8,256,768]{2,1,0:T(8,128)} %fusion.9), calls=%async_computation.1 | async-start | bytes 12582912 | tf_op jit(solution)/shard_map/all_to_all | solution.py:307
  213.7 322.5 %all-reduce.5.cloned.1.call-start = ((), (), s32[]{:S(2)}) async-start(), calls=%async_computation.6 | async-start | bytes 9437184 | tf_op jit(solution)/shard_map/psum | solution.py:299
  219.6 2.2 copy-start
  221.8 2.6 copy-start.8
  221.8 6.5 %slice-start = ((s8[4718592]{0:T(1024)(128)(4,1)}), s8[4194304]{0:T(1024)(128)(4,1)S(1)}, s32[]{:S(2)}) async-start(s8[4718592]{0:T(1024)(128)(4,1)} %bitcast.115), calls=%async_computation.8 | async-start | bytes 8388608
  224.4 4.0 slice-start.1
  362.1 1.7 copy-start.9
  408.1 1.4 copy-start.1
  546.4 9.9 %copy-start.2 = (f32[768,768]{1,0:T(8,128)S(1)}, f32[768,768]{1,0:T(8,128)}, u32[]{:S(2)}) copy-start(f32[768,768]{1,0:T(8,128)} %copy-done.1) | copy-start | bytes 7077892
  565.4 10.6 %copy-start.7 = (f32[768,768]{1,0:T(8,128)S(1)}, f32[768,768]{1,0:T(8,128)}, u32[]{:S(2)}) copy-start(f32[768,768]{1,0:T(8,128)} %copy.38) | copy-start | bytes 7077892
Sparse Core Ops, SparseCore 0:
  10.1 42.8 all-gather.5
  54.6 37.6 all-gather.7
  126.5 69.9 all-reduce.2
  198.7 140.4 all-gather.11
  340.7 21.3 all-gather.9
  366.6 169.6 all-reduce.4
